TPU v7x, 32 devices: a whole 2x2x4 slice. The times are simulated.
32 devices in a mesh: shard: 2 (over x), tm: 16 (over z, y, core).
Axes of the slice: x: 2, y: 2, z: 4, core: 2. Of those that a mesh axis runs over, the one named last changes fastest.
Arguments:
- latents: bfloat16 [128, 32, 1536], P(('shard', 'tm')), parts along dimension 0, as said below
- w_query: bfloat16 [1536, 1536], replicated, may hold values from -0.15625 to 0.15625
- w_key: bfloat16 [1536, 1536], replicated, may hold values from -0.15625 to 0.15625
- w_value: bfloat16 [1536, 1536], replicated, may hold values from -0.15625 to 0.15625
- w_out: bfloat16 [1536, 1536], replicated, may hold values from -0.15625 to 0.15625
- cotangent: bfloat16 [128, 32, 1536], P(('shard', 'tm')), parts along dimension 0, may hold values from -6 to 6
- memory_ids: int32 [128, 4], P(('shard', 'tm')), parts along dimension 0, may hold values from 0 to 63, as said below
- memory_count: int32 [128], P(('shard', 'tm')), parts along dimension 0, may hold values from 1 to 4
- tile_mask: int32 [128, 2], P(('shard', 'tm')), parts along dimension 0, may hold values 0 or 1
Outputs:
- layer_out: bfloat16 [128, 32, 1536], P(('shard', 'tm')), parts along dimension 0
- latent_grad: bfloat16 [128, 32, 1536], P(('shard', 'tm')), parts along dimension 0
There are 2 independent parts, one for each index of `shard`. A program takes and returns all parts, laid end to end along the dimension named above; an argument that names none is the same for every part. Nothing has to cross between parts.
Inputs may be any that keep to these rules, and one draw needn't show every extreme that they name: `memory_ids`: the 16 entries of the frames of one aligned block of 4 frames (frames b * 4 to b * 4 + 3) lie in 16 different such blocks. `latents`: entries lie between -40 and 40.
All inputs are finite; a program needn't handle non-finite values. No bound on the sum of `tile_mask` on one device may be relied on, other than what follows from the above.
Results may differ from a plain program's by a relative error of at most 0.014.
The roundings to bfloat16 on the way count: a program that leaves them out, or rounds other values in their place, can miss the bound.
Values may be sent and summed in bfloat16 or wider, within the bound.
A program may use at most 192 MiB of HBM per device.

v0:
```python
import functools
import math

import jax
import jax.numpy as jnp
from jax import lax
from jax.experimental import pallas as pl
from jax.experimental.pallas import tpu as pltpu
from jax.sharding import PartitionSpec as P

HEADS = 24
GROUP = 4
NT = (((1,), (1,)), ((), ()))
NN = (((1,), (0,)), ((), ()))
TN = (((0,), (0,)), ((), ()))


def dot(a, b, dims):
    return lax.dot_general(a, b, dims, preferred_element_type=jnp.float32)


def attend_kernel(
    owners, valid, q_ref, g_ref, k_ext, v_ext, k_mem, v_mem,
    mixed_ref, dq_ref, sums_ref, edge_ref, slots_ref,
    *, frames, mem, tile, head_dim, spare,
):
    width = q_ref.shape[1]
    rows = GROUP * tile
    inv_root = 1.0 / math.sqrt(head_dim)
    own_head = (
        lax.broadcasted_iota(jnp.int32, (rows, width), 0) // tile
        == lax.broadcasted_iota(jnp.int32, (rows, width), 1) // head_dim
    )

    def spread(block):
        tall = jnp.concatenate([block] * GROUP, axis=0)
        return jnp.where(own_head, tall, jnp.zeros_like(tall))

    def fold(tall):
        tall = jnp.where(own_head, tall, 0.0)
        total = tall[0:tile]
        for part in range(1, GROUP):
            total = total + tall[part * tile : (part + 1) * tile]
        return total

    if spare:
        slots_ref[...] = jnp.zeros_like(slots_ref)
    for f in range(frames):
        here = slice(f * tile, (f + 1) * tile)
        near = slice(f * tile, (f + 3) * tile)
        spots = [owners[f * mem + j] for j in range(mem)]

        def gather(ext, far):
            return jnp.concatenate([ext[near, :]] + [far[s] for s in spots], axis=0)

        keys = gather(k_ext, k_mem)
        values = gather(v_ext, v_mem)
        queries = spread(q_ref[here, :])
        grads = spread(g_ref[here, :])
        scores = dot(queries, keys, NT) * inv_root
        scores = jnp.where(valid[f : f + 1, :] > 0.5, scores, -1e30)
        expo = jnp.exp(scores - jnp.max(scores, axis=-1, keepdims=True))
        prob = expo / jnp.sum(expo, axis=-1, keepdims=True)
        low = prob.astype(jnp.bfloat16)
        mixed_ref[here, :] = fold(dot(low, values, NN)).astype(jnp.bfloat16)
        prob_grad = dot(grads, values, NT)
        delta = jnp.sum(prob * prob_grad, axis=-1, keepdims=True)
        score_grad = (prob * (prob_grad - delta) * inv_root).astype(jnp.bfloat16)
        dq_ref[here, :] = fold(dot(score_grad, keys, NN)).astype(jnp.bfloat16)
        parts = (
            dot(score_grad, queries, TN).astype(jnp.bfloat16),
            dot(low, grads, TN).astype(jnp.bfloat16),
        )
        for kv, part in enumerate(parts):
            before = part[0:tile]
            own = part[tile : 2 * tile].astype(jnp.float32)
            after = part[2 * tile : 3 * tile]
            if f == 0:
                edge_ref[0, kv] = before
                sums_ref[kv, here, :] = own
            else:
                back = slice((f - 1) * tile, f * tile)
                sums_ref[kv, back, :] += before.astype(jnp.float32)
                sums_ref[kv, here, :] += own
            if f == frames - 1:
                edge_ref[1, kv] = after
            else:
                sums_ref[kv, (f + 1) * tile : (f + 2) * tile, :] = after.astype(jnp.float32)
            for j in range(mem):
                slots_ref[spots[j], kv] = part[(3 + j) * tile : (4 + j) * tile]


def finish_kernel(
    asked, dq_ref, sums_ref, below_ref, above_ref, back_ref, wq_ref, wk_ref, wv_ref,
    out_ref, acc, total, *, frames, tile,
):
    step = pl.program_id(0)
    acc[...] = sums_ref[...]
    last = slice((frames - 1) * tile, frames * tile)
    for kv in range(2):
        acc[kv, 0:tile, :] += below_ref[kv].astype(jnp.float32)
        acc[kv, last, :] += above_ref[kv].astype(jnp.float32)

    @pl.loop(0, back_ref.shape[0])
    def _(n):
        @pl.when(asked[n] >= 0)
        def _():
            spot = pl.ds(pl.multiple_of(asked[n] * tile, tile), tile)
            for kv in range(2):
                acc[kv, spot, :] += back_ref[n, kv].astype(jnp.float32)

    @pl.when(step == 0)
    def _():
        total[...] = jnp.zeros_like(total)

    total[...] += (
        dot(dq_ref[...], wq_ref[...], NT)
        + dot(acc[0].astype(jnp.bfloat16), wk_ref[...], NT)
        + dot(acc[1].astype(jnp.bfloat16), wv_ref[...], NT)
    )

    @pl.when(step == pl.num_programs(0) - 1)
    def _():
        out_ref[...] = total[...].astype(jnp.bfloat16)


def on_device(
    latents, w_query, w_key, w_value, w_out, cotangent, memory_ids, memory_count, tile_mask
):
    frames, tile, width = latents.shape
    count = lax.axis_size("tm")
    me = lax.axis_index("tm")
    rows = latents.reshape(-1, width)
    mem = memory_ids.shape[1]
    inner = w_query.shape[1]
    head_dim = inner // HEADS
    cols = GROUP * head_dim
    steps = inner // cols
    up = [(i, i + 1) for i in range(count - 1)]
    down = [(i + 1, i) for i in range(count - 1)]

    owners = (memory_ids // frames).reshape(-1).astype(jnp.int32)
    local = (memory_ids % frames).reshape(-1).astype(jnp.int32)
    peers = jnp.arange(count, dtype=jnp.int32)
    matched = owners[None, :] == peers[:, None]
    wanted = jnp.where(
        jnp.any(matched, axis=1), jnp.sum(jnp.where(matched, local[None, :], 0), axis=1), -1
    )
    asked = lax.all_to_all(wanted[:, None], "tm", split_axis=0, concat_axis=0, tiled=True)[:, 0]
    frame_ids = jnp.arange(frames, dtype=jnp.int32)
    selector = (asked[:, None] == frame_ids[None, :]).astype(jnp.bfloat16)
    outgoing = jnp.einsum(
        "nf,ftc->ntc", selector, latents, preferred_element_type=jnp.float32
    ).astype(jnp.bfloat16)
    received = lax.all_to_all(outgoing, "tm", split_axis=0, concat_axis=0, tiled=True)
    below_rows = lax.ppermute(latents[frames - 1], "tm", up)
    above_rows = lax.ppermute(latents[0], "tm", down)

    def project(block, weight):
        return jnp.dot(block, weight, preferred_element_type=jnp.float32).astype(jnp.bfloat16)

    ext_rows = jnp.concatenate([below_rows, rows, above_rows], axis=0)
    queries = project(rows, w_query)
    k_ext = project(ext_rows, w_key)
    v_ext = project(ext_rows, w_value)
    out_grad = lax.dot_general(
        cotangent.reshape(-1, width), w_out, NT, preferred_element_type=jnp.float32
    ).astype(jnp.bfloat16)
    far_rows = received.reshape(count * tile, width)
    k_mem = project(far_rows, w_key).reshape(count, tile, inner)
    v_mem = project(far_rows, w_value).reshape(count, tile, inner)

    global_ids = me * frames + frame_ids
    lower = (tile_mask[:, 0] * (global_ids >= 1)).astype(jnp.float32)
    upper = (tile_mask[:, 1] * (global_ids < frames * count - 1)).astype(jnp.float32)
    kept = (jnp.arange(mem, dtype=jnp.int32)[None, :] < memory_count[:, None]).astype(jnp.float32)
    valid = jnp.concatenate(
        [lower[:, None], jnp.ones((frames, 1), jnp.float32), upper[:, None], kept], axis=1
    )
    valid = jnp.repeat(valid, tile, axis=1)

    own = frames * tile
    flat = lambda n: pl.BlockSpec((n, cols), lambda g, *_: (0, g))
    deep = lambda n: pl.BlockSpec((n, tile, cols), lambda g, *_: (0, 0, g))
    mixed, query_grad, sums, edges, slots = pl.pallas_call(
        functools.partial(
            attend_kernel, frames=frames, mem=mem, tile=tile, head_dim=head_dim,
            spare=count > frames * mem,
        ),
        grid_spec=pltpu.PrefetchScalarGridSpec(
            num_scalar_prefetch=1,
            grid=(steps,),
            in_specs=[
                pl.BlockSpec(valid.shape, lambda g, *_: (0, 0)),
                flat(own), flat(own), flat(own + 2 * tile), flat(own + 2 * tile),
                deep(count), deep(count),
            ],
            out_specs=[
                flat(own), flat(own),
                pl.BlockSpec((2, own, cols), lambda g, *_: (0, 0, g)),
                pl.BlockSpec((2, 2, tile, cols), lambda g, *_: (0, 0, 0, g)),
                pl.BlockSpec((count, 2, tile, cols), lambda g, *_: (0, 0, 0, g)),
            ],
        ),
        out_shape=[
            jax.ShapeDtypeStruct((own, inner), jnp.bfloat16),
            jax.ShapeDtypeStruct((own, inner), jnp.bfloat16),
            jax.ShapeDtypeStruct((2, own, inner), jnp.float32),
            jax.ShapeDtypeStruct((2, 2, tile, inner), jnp.bfloat16),
            jax.ShapeDtypeStruct((count, 2, tile, inner), jnp.bfloat16),
        ],
        compiler_params=pltpu.CompilerParams(vmem_limit_bytes=40 * 2**20),
    )(owners, valid, queries, out_grad, k_ext, v_ext, k_mem, v_mem)

    from_below = lax.ppermute(edges[1], "tm", up)
    from_above = lax.ppermute(edges[0], "tm", down)
    back = lax.all_to_all(slots, "tm", split_axis=0, concat_axis=0, tiled=True)
    layer_out = project(mixed, w_out).reshape(frames, tile, width)
    weight = pl.BlockSpec((width, cols), lambda g, *_: (0, g))
    side = pl.BlockSpec((2, tile, cols), lambda g, *_: (0, 0, g))
    latent_grad = pl.pallas_call(
        functools.partial(finish_kernel, frames=frames, tile=tile),
        grid_spec=pltpu.PrefetchScalarGridSpec(
            num_scalar_prefetch=1,
            grid=(steps,),
            in_specs=[
                flat(own),
                pl.BlockSpec((2, own, cols), lambda g, *_: (0, 0, g)),
                side, side,
                pl.BlockSpec((count, 2, tile, cols), lambda g, *_: (0, 0, 0, g)),
                weight, weight, weight,
            ],
            out_specs=pl.BlockSpec((own, width), lambda g, *_: (0, 0)),
            scratch_shapes=[
                pltpu.VMEM((2, own, cols), jnp.float32),
                pltpu.VMEM((own, width), jnp.float32),
            ],
        ),
        out_shape=jax.ShapeDtypeStruct((own, width), jnp.bfloat16),
        compiler_params=pltpu.CompilerParams(vmem_limit_bytes=40 * 2**20),
    )(asked, query_grad, sums, from_below, from_above, back, w_query, w_key, w_value)
    return (layer_out, latent_grad.reshape(frames, tile, width))


def solution(mesh):
    placed = (
        P(("shard", "tm"), None, None),
        P(),
        P(),
        P(),
        P(),
        P(("shard", "tm"), None, None),
        P(("shard", "tm"), None),
        P(("shard", "tm")),
        P(("shard", "tm"), None),
    )
    return jax.shard_map(
        on_device,
        mesh=mesh,
        in_specs=placed,
        out_specs=(P(("shard", "tm"), None, None), P(("shard", "tm"), None, None)),
        check_vma=False,
    )
```

profile of v0, /device:TPU:16, one launch (start us, length us, event | category | flops | bytes accessed | tf_op | source)
XLA Modules:
  0.0 194.5 jit_solution(3491359807743097779)
XLA Ops:
  1.9 10.1 %all_to_all.16 = s32[16,1,1]{2,1,0:T(1,128)S(1)} all-to-all(s32[16,1,1]{2,1,0:T(1,128)S(1)} %copy.30), channel_id=1, replica_groups=mesh['shard'=2,'tm'=16] {'tm'}, dimensions={0} | all-to-all | bytes 128 | tf_op jit(solution)/shard_map/all_to_all | solution.py:149
  12.3 1.7 convolution_convert_fusion.2
  14.0 2.0 %copy.32 = bf16[16,32,1536]{2,1,0:T(8,128)(2,1)} copy(bf16[16,32,1536]{2,0,1:T(8,128)(2,1)S(1)} %convolution_convert_fusion.2) | data formatting | bytes 3145728 | tf_op jit(solution)/shard_map/convert_element_type | solution.py:154
  16.0 6.6 %all-to-all-start.1 = ((bf16[16,32,1536]{2,1,0:T(8,128)(2,1)}), bf16[16,32,1536]{2,1,0:T(8,128)(2,1)}, u32[]{:S(2)}, u32[]{:S(2)}) async-start(bf16[16,32,1536]{2,1,0:T(8,128)(2,1)} %copy.32), calls=%async_computation.1 | async-start | bytes 3145728 | tf_op jit(solution)/shard_map/all_to_all | solution.py:155
  22.7 2.1 %collective-permute-start = (bf16[32,1536]{1,0:T(8,128)(2,1)S(1)}, bf16[32,1536]{1,0:T(8,128)(2,1)S(1)}, u32[]{:S(2)}, u32[]{:S(2)}) collective-permute-start(bf16[32,1536]{1,0:T(8,128)(2,1)S(1)} %get-tuple-element.14), channel_id=1, source_target_pairs={{0,1},{1,2},{2,3},{3,4},{4,5},{5,6},{6,7},{7,8},{8,9},{9,10},{10,1... | collective-permute-start | bytes 294920 | tf_op jit(solution)/shard_map/ppermute | solution.py:156
  24.7 4.4 %collective-permute-start.1 = (bf16[32,1536]{1,0:T(8,128)(2,1)S(1)}, bf16[32,1536]{1,0:T(8,128)(2,1)S(1)}, u32[]{:S(2)}, u32[]{:S(2)}) collective-permute-start(bf16[32,1536]{1,0:T(8,128)(2,1)S(1)} %get-tuple-element.15), channel_id=1, source_target_pairs={{1,0},{2,1},{3,2},{4,3},{5,4},{6,5},{7,6},{8,7},{9,8},{10,9},{11,1... | collective-permute-start | bytes 294920 | tf_op jit(solution)/shard_map/ppermute | solution.py:157
  29.5 4.0 %convolution_convert_fusion.6.g_ref = bf16[128,1536]{1,0:T(8,128)(2,1)S(1)} fusion(bf16[128,1536]{1,0:T(8,128)(2,1)S(1)} %bitcast.33, bf16[1536,1536]{1,0:T(8,128)(2,1)} %param.13), kind=kOutput, calls=%fused_computation.6 | convolution fusion | flops 604176384 | bytes 5505024 | tf_op jit(solution)/shard_map/dot_general | solution.py:166
  33.5 3.1 %convolution_convert_fusion.7.q_ref = bf16[128,1536]{1,0:T(8,128)(2,1)S(1)} fusion(bf16[128,1536]{1,0:T(8,128)(2,1)S(1)} %bitcast.36, bf16[1536,1536]{1,0:T(8,128)(2,1)} %wq_ref.1), kind=kOutput, calls=%fused_computation.7 | convolution fusion | flops 604176384 | bytes 5505024 | tf_op jit(solution)/shard_map/dot_general | solution.py:160
  36.8 23.3 %collective-permute-done = bf16[32,1536]{1,0:T(8,128)(2,1)S(1)} collective-permute-done((bf16[32,1536]{1,0:T(8,128)(2,1)S(1)}, bf16[32,1536]{1,0:T(8,128)(2,1)S(1)}, u32[]{:S(2)}, u32[]{:S(2)}) %collective-permute-start) | collective-permute-done | bytes 98336 | tf_op jit(solution)/shard_map/ppermute | solution.py:156
  60.1 3.4 %convolution_convert_fusion.3.v_ext = bf16[192,1536]{1,0:T(8,128)(2,1)S(1)} fusion(bf16[1536,1536]{1,0:T(8,128)(2,1)} %wv_ref.1, bf16[32,1536]{1,0:T(8,128)(2,1)S(1)} %collective-permute-done.1, bf16[128,1536]{1,0:T(8,128)(2,1)S(1)} %bitcast.37, bf16[32,1536]{1,0:T(8,128)(2,1)S(1)} %collective-permute-done), kind=kOutput, calls=%fused_computation.3 | convolution fusion | flops 908034048 | bytes 5898240 | tf_op jit(solution)/shard_map/dot_general | solution.py:160
  63.5 3.4 %convolution_convert_fusion.4.k_ext = bf16[192,1536]{1,0:T(8,128)(2,1)S(1)} fusion(bf16[1536,1536]{1,0:T(8,128)(2,1)} %wk_ref.1, bf16[32,1536]{1,0:T(8,128)(2,1)S(1)} %collective-permute-done.1, bf16[128,1536]{1,0:T(8,128)(2,1)S(1)} %bitcast.38, bf16[32,1536]{1,0:T(8,128)(2,1)S(1)} %collective-permute-done), kind=kOutput, calls=%fused_computation.4 | convolution fusion | flops 908034048 | bytes 5898240 | tf_op jit(solution)/shard_map/dot_general | solution.py:160
  67.0 5.4 %convolution_convert_fusion = bf16[512,1536]{1,0:T(8,128)(2,1)S(1)} fusion(bf16[512,1536]{1,0:T(8,128)(2,1)} %bitcast.6, bf16[1536,1536]{1,0:T(8,128)(2,1)} %wv_ref.1), kind=kOutput, calls=%fused_computation | convolution fusion | flops 2416705536 | bytes 7864320 | tf_op jit(solution)/shard_map/dot_general | solution.py:160
  72.4 5.4 %convolution_convert_fusion.1 = bf16[512,1536]{1,0:T(8,128)(2,1)S(1)} fusion(bf16[512,1536]{1,0:T(8,128)(2,1)} %bitcast.6, bf16[1536,1536]{1,0:T(8,128)(2,1)} %wk_ref.1), kind=kOutput, calls=%fused_computation.1 | convolution fusion | flops 2416705536 | bytes 7864320 | tf_op jit(solution)/shard_map/dot_general | solution.py:160
  77.8 16.8 %shard_map.104 = (bf16[128,1536]{1,0:T(8,128)(2,1)S(1)}, bf16[128,1536]{1,0:T(8,128)(2,1)S(1)}, f32[2,128,1536]{2,1,0:T(8,128)S(1)}, bf16[2,2,32,1536]{3,2,1,0:T(8,128)(2,1)S(1)}, bf16[16,2,32,1536]{3,2,1,0:T(8,128)(2,1)S(1)}) custom-call(s32[16]{0:T(128)S(1)} %reshape.67.owners, f32[4,224]{1,0:T(4,128)S(1)} %reshape.68.valid, ...), custom_call_target="tpu_custom_call" | custom-call | tf_op jit(solution)/shard_map/pallas_call | solution.py:185
  94.6 1.6 copy-done.2
  96.2 1.2 copy-done.3
  99.6 4.2 %all-to-all-start.2 = ((bf16[16,2,32,1536]{3,2,1,0:T(8,128)(2,1)}), bf16[16,2,32,1536]{3,2,1,0:T(8,128)(2,1)S(1)}, u32[]{:S(2)}, u32[]{:S(2)}) async-start(bf16[16,2,32,1536]{3,2,1,0:T(8,128)(2,1)} %copy-done.2), calls=%async_computation.2 | async-start | bytes 6291456 | tf_op jit(solution)/shard_map/all_to_all | solution.py:217
  104.9 3.1 %collective-permute-start.3 = (bf16[2,32,1536]{2,1,0:T(8,128)(2,1)S(1)}, bf16[2,32,1536]{2,1,0:T(8,128)(2,1)S(1)}, u32[]{:S(2)}, u32[]{:S(2)}) collective-permute-start(bf16[2,32,1536]{2,1,0:T(8,128)(2,1)S(1)} %get-tuple-element.12), channel_id=1, source_target_pairs={{1,0},{2,1},{3,2},{4,3},{5,4},{6,5},{7,6},{8,7},{9,8},{10,9},{11,1... | collective-permute-start | bytes 589832 | tf_op jit(solution)/shard_map/ppermute | solution.py:216
  108.0 1.9 collective-permute-start.2
  110.0 4.0 %convolution_convert_fusion.5 = bf16[128,1536]{1,0:T(8,128)(2,1)} fusion(bf16[128,1536]{1,0:T(8,128)(2,1)} %copy-done.8, bf16[1536,1536]{1,0:T(8,128)(2,1)} %param.13), kind=kOutput, calls=%fused_computation.5 | convolution fusion | flops 604176384 | bytes 5505024 | tf_op jit(solution)/shard_map/dot_general | solution.py:160
  114.0 60.3 %collective-permute-done.3.above_ref = bf16[2,32,1536]{2,1,0:T(8,128)(2,1)S(1)} collective-permute-done((bf16[2,32,1536]{2,1,0:T(8,128)(2,1)S(1)}, bf16[2,32,1536]{2,1,0:T(8,128)(2,1)S(1)}, u32[]{:S(2)}, u32[]{:S(2)}) %collective-permute-start.3) | collective-permute-done | bytes 196640 | tf_op jit(solution)/shard_map/ppermute | solution.py:216
  176.8 2.3 %copy-done.1 = bf16[1536,1536]{1,0:T(8,128)(2,1)S(1)} copy-done((bf16[1536,1536]{1,0:T(8,128)(2,1)S(1)}, bf16[1536,1536]{1,0:T(8,128)(2,1)}, u32[]{:S(2)}) %copy-start.1) | copy-done | bytes 4718616
  179.1 1.4 copy-done.4
  183.4 11.1 %shard_map.105 = bf16[128,1536]{1,0:T(8,128)(2,1)} custom-call(s32[16]{0:T(128)S(1)} %reduce.asked, bf16[128,1536]{1,0:T(8,128)(2,1)S(1)} %copy-done.7, f32[2,128,1536]{2,1,0:T(8,128)S(1)} %copy-done.4, bf16[2,32,1536]{2,1,0:T(8,128)(2,1)S(1)} %copy-done.12, bf16[2,32,1536]{2,1,0:T(8,128)(2,1)S(1)} %copy-done.10, ...), custom_call_target="tpu_custom_call" | custom-call | tf_op jit(solution)/shard_map/pallas_call | solution.py:221
  (50 shorter events, 10.9 us)
Async XLA Ops:
  0.6 28.9 %copy-start = (bf16[4,32,1536]{2,1,0:T(8,128)(2,1)S(1)}, bf16[4,32,1536]{2,1,0:T(8,128)(2,1)}, u32[]{:S(2)}) copy-start(bf16[4,32,1536]{2,1,0:T(8,128)(2,1)} %param.14) | copy-start | bytes 1179652
  14.0 8.6 %copy-start.13 = (bf16[4,32,1536]{2,1,0:T(8,128)(2,1)S(1)}, bf16[4,32,1536]{2,1,0:T(8,128)(2,1)}, u32[]{:S(2)}) copy-start(bf16[4,32,1536]{2,1,0:T(8,128)(2,1)} %param.9) | copy-start | bytes 1179652
  14.0 15.1 %copy-start.14 = (s32[4,2]{0,1:T(2,128)S(1)}, s32[4,2]{0,1:T(2,128)}, u32[]{:S(2)}) copy-start(s32[4,2]{0,1:T(2,128)} %param.17) | copy-start | bytes 100
  14.0 15.4 %copy-start.15 = (s32[4]{0:T(128)S(1)}, s32[4]{0:T(128)}, u32[]{:S(2)}) copy-start(s32[4]{0:T(128)} %param.16) | copy-start | bytes 52
  16.0 50.9 %all-to-all-start.1 = ((bf16[16,32,1536]{2,1,0:T(8,128)(2,1)}), bf16[16,32,1536]{2,1,0:T(8,128)(2,1)}, u32[]{:S(2)}, u32[]{:S(2)}) async-start(bf16[16,32,1536]{2,1,0:T(8,128)(2,1)} %copy.32), calls=%async_computation.1 | async-start | bytes 3145728 | tf_op jit(solution)/shard_map/all_to_all | solution.py:155
  22.7 37.4 %collective-permute-start = (bf16[32,1536]{1,0:T(8,128)(2,1)S(1)}, bf16[32,1536]{1,0:T(8,128)(2,1)S(1)}, u32[]{:S(2)}, u32[]{:S(2)}) collective-permute-start(bf16[32,1536]{1,0:T(8,128)(2,1)S(1)} %get-tuple-element.14), channel_id=1, source_target_pairs={{0,1},{1,2},{2,3},{3,4},{4,5},{5,6},{6,7},{7,8},{8,9},{9,10},{10,1... | collective-permute-start | bytes 294920 | tf_op jit(solution)/shard_map/ppermute | solution.py:156
  24.7 35.4 %collective-permute-start.1 = (bf16[32,1536]{1,0:T(8,128)(2,1)S(1)}, bf16[32,1536]{1,0:T(8,128)(2,1)S(1)}, u32[]{:S(2)}, u32[]{:S(2)}) collective-permute-start(bf16[32,1536]{1,0:T(8,128)(2,1)S(1)} %get-tuple-element.15), channel_id=1, source_target_pairs={{1,0},{2,1},{3,2},{4,3},{5,4},{6,5},{7,6},{8,7},{9,8},{10,9},{11,1... | collective-permute-start | bytes 294920 | tf_op jit(solution)/shard_map/ppermute | solution.py:157
  94.6 1.7 copy-start.2
  96.2 1.2 copy-start.3
  97.4 0.7 copy-start.5
  98.1 0.7 copy-start.6
  98.9 0.7 copy-start.8
  99.6 77.1 %all-to-all-start.2 = ((bf16[16,2,32,1536]{3,2,1,0:T(8,128)(2,1)}), bf16[16,2,32,1536]{3,2,1,0:T(8,128)(2,1)S(1)}, u32[]{:S(2)}, u32[]{:S(2)}) async-start(bf16[16,2,32,1536]{3,2,1,0:T(8,128)(2,1)} %copy-done.2), calls=%async_computation.2 | async-start | bytes 6291456 | tf_op jit(solution)/shard_map/all_to_all | solution.py:217
  104.9 69.4 %collective-permute-start.3 = (bf16[2,32,1536]{2,1,0:T(8,128)(2,1)S(1)}, bf16[2,32,1536]{2,1,0:T(8,128)(2,1)S(1)}, u32[]{:S(2)}, u32[]{:S(2)}) collective-permute-start(bf16[2,32,1536]{2,1,0:T(8,128)(2,1)S(1)} %get-tuple-element.12), channel_id=1, source_target_pairs={{1,0},{2,1},{3,2},{4,3},{5,4},{6,5},{7,6},{8,7},{9,8},{10,9},{11,1... | collective-permute-start | bytes 589832 | tf_op jit(solution)/shard_map/ppermute | solution.py:216
  108.0 68.0 %collective-permute-start.2 = (bf16[2,32,1536]{2,1,0:T(8,128)(2,1)S(1)}, bf16[2,32,1536]{2,1,0:T(8,128)(2,1)S(1)}, u32[]{:S(2)}, u32[]{:S(2)}) collective-permute-start(bf16[2,32,1536]{2,1,0:T(8,128)(2,1)S(1)} %get-tuple-element.13), channel_id=1, source_target_pairs={{0,1},{1,2},{2,3},{3,4},{4,5},{5,6},{6,7},{7,8},{8,9},{9,10},{10,1... | collective-permute-start | bytes 589832 | tf_op jit(solution)/shard_map/ppermute | solution.py:215
  174.3 0.7 copy-start.9
  176.1 0.7 copy-start.11
  176.8 2.3 %copy-start.1 = (bf16[1536,1536]{1,0:T(8,128)(2,1)S(1)}, bf16[1536,1536]{1,0:T(8,128)(2,1)}, u32[]{:S(2)}) copy-start(bf16[1536,1536]{1,0:T(8,128)(2,1)} %wq_ref.1) | copy-start | bytes 14155780
  179.1 1.4 copy-start.4
  180.5 1.0 copy-start.7
  181.5 0.9 copy-start.10
  182.4 0.9 copy-start.12
where the time goes:
time: 196 us; the launch traced here: 194 us
  waiting for transfers between devices  84.7 us (43%)
  matrix products  30.4 us (16%)
  Pallas kernels  27.9 us (14%)
  starting transfers between devices  22.3 us (11%)
  local copies, waits for them, and re-layouts  16.8 us (9%)
  blocking collectives  10.1 us (5%)
    ppermute x1, waiting for transfers between devices, on_device(): from_above = lax.ppermute(edges[0], 'tm', down)  60.3 us
    dot_general x6, matrix products, project(): jnp.dot(block, weight, preferred_element_type=jnp.float32)  24.8 us
    ppermute x1, waiting for transfers between devices, on_device(): below_rows = lax.ppermute(latents[frames - 1], 'tm', up)  23.3 us
    pallas_call x1, Pallas kernels, on_device(): pl.pallas_call(functools.partial(attend_kernel, frames=frames, mem=mem, t...  16.8 us
    unnamed x32, local copies, waits for them, and re-layouts  13 us
    pallas_call x1, Pallas kernels, on_device(): pl.pallas_call(functools.partial(finish_kernel, frames=frames, tile=tile)...  11.1 us
    all_to_all x1, blocking collectives, on_device(): lax.all_to_all(wanted[:, None], 'tm', split_axis=0, concat_axis=0, tiled=...  10.1 us
    all_to_all x1, starting transfers between devices, on_device(): lax.all_to_all(outgoing, 'tm', split_axis=0, concat_axis=0, tiled=True)  6.6 us
  transfers between devices with their start and end apart: 6, of which 3 were waited for; matrix products, arithmetic and copies ran while one was open for 10% of the time, Pallas kernels for 0%

commit v1 on v0

v1 whole, which is shorter than its diff:
```python
import functools
import math

import jax
import jax.numpy as jnp
from jax import lax
from jax.experimental import pallas as pl
from jax.experimental.pallas import tpu as pltpu
from jax.sharding import PartitionSpec as P

HEADS = 24
GROUP = 4
NT = (((1,), (1,)), ((), ()))
NN = (((1,), (0,)), ((), ()))
TN = (((0,), (0,)), ((), ()))
MESH = pl.DeviceIdType.MESH


def dot(a, b, dims):
    return lax.dot_general(a, b, dims, preferred_element_type=jnp.float32)


def attend_kernel(
    count, frames, mem, tile, head_dim, steps,
    owners, place, valid, pick, q_ref, g_ref, k_ext, v_ext, k_mem, v_mem,
    wo_hbm, wq_hbm, wk_hbm, wv_hbm,
    layer_ref, grad_ref,
    weights, mixed, query_grad, sums, blocks, outgoing, incoming, total,
    weight_sem, send_sem, recv_sem, edge_send, edge_recv,
):
    me = lax.axis_index("tm")
    width = q_ref.shape[1]
    cols = width // steps
    rows = GROUP * tile
    inv_root = 1.0 / math.sqrt(head_dim)
    loads = [
        pltpu.make_async_copy(source, weights.at[i], weight_sem.at[i])
        for i, source in enumerate((wo_hbm, wq_hbm, wk_hbm, wv_hbm))
    ]
    for load in loads:
        load.start()

    barrier = pltpu.get_barrier_semaphore()

    @pl.loop(1, count)
    def _(d):
        pl.semaphore_signal(
            barrier, inc=1, device_id={"tm": lax.rem(me + d, count)}, device_id_type=MESH
        )

    own_head = (
        lax.broadcasted_iota(jnp.int32, (rows, cols), 0) // tile
        == lax.broadcasted_iota(jnp.int32, (rows, cols), 1) // head_dim
    )

    def spread(block):
        tall = jnp.concatenate([block] * GROUP, axis=0)
        return jnp.where(own_head, tall, jnp.zeros_like(tall))

    def fold(tall):
        tall = jnp.where(own_head, tall, 0.0)
        flat = tall[0:tile]
        for part in range(1, GROUP):
            flat = flat + tall[part * tile : (part + 1) * tile]
        return flat

    def push(g, d):
        return pltpu.make_async_remote_copy(
            src_ref=outgoing.at[g, d],
            dst_ref=incoming.at[g, d],
            send_sem=send_sem.at[g],
            recv_sem=recv_sem.at[g],
            device_id={"tm": lax.rem(me + d, count)},
            device_id_type=MESH,
        )

    def push_edge(g, side):
        return pltpu.make_async_remote_copy(
            src_ref=outgoing.at[g, count + side],
            dst_ref=incoming.at[g, count + side],
            send_sem=edge_send.at[g, side],
            recv_sem=edge_recv.at[g, side],
            device_id={"tm": lax.rem(me + (1 if side == 0 else count - 1), count)},
            device_id_type=MESH,
        )

    def attend(g):
        lanes = pl.ds(pl.multiple_of(g * cols, cols), cols)
        for f in range(frames):
            here = slice(f * tile, (f + 1) * tile)
            near = slice(f * tile, (f + 3) * tile)

            def gather(ext, far):
                return jnp.concatenate(
                    [ext[near, lanes]] + [far[owners[f * mem + j], :, lanes] for j in range(mem)],
                    axis=0,
                )

            keys = gather(k_ext, k_mem)
            values = gather(v_ext, v_mem)
            queries = spread(q_ref[here, lanes])
            grads = spread(g_ref[here, lanes])
            scores = dot(queries, keys, NT) * inv_root
            scores = jnp.where(valid[f : f + 1, :] > 0.5, scores, -1e30)
            expo = jnp.exp(scores - jnp.max(scores, axis=-1, keepdims=True))
            prob = expo / jnp.sum(expo, axis=-1, keepdims=True)
            low = prob.astype(jnp.bfloat16)
            mixed[here, lanes] = fold(dot(low, values, NN)).astype(jnp.bfloat16)
            prob_grad = dot(grads, values, NT)
            delta = jnp.sum(prob * prob_grad, axis=-1, keepdims=True)
            score_grad = (prob * (prob_grad - delta) * inv_root).astype(jnp.bfloat16)
            query_grad[here, lanes] = fold(dot(score_grad, keys, NN)).astype(jnp.bfloat16)
            parts = (
                dot(score_grad, queries, TN).astype(jnp.bfloat16),
                dot(low, grads, TN).astype(jnp.bfloat16),
            )
            for kv, part in enumerate(parts):
                before = part[0:tile]
                own = part[tile : 2 * tile].astype(jnp.float32)
                after = part[2 * tile : 3 * tile]
                if f == 0:
                    outgoing[g, count + 1, kv] = before
                    sums[kv, here, lanes] = own
                else:
                    back = slice((f - 1) * tile, f * tile)
                    sums[kv, back, lanes] += before.astype(jnp.float32)
                    sums[kv, here, lanes] += own
                if f == frames - 1:
                    outgoing[g, count, kv] = after
                else:
                    ahead = slice((f + 1) * tile, (f + 2) * tile)
                    sums[kv, ahead, lanes] = after.astype(jnp.float32)
                for j in range(mem):
                    blocks[f * mem + j, kv] = part[(3 + j) * tile : (4 + j) * tile]

    def send(g):
        @pl.loop(1, count)
        def _(d):
            outgoing[g, d] = blocks[place[lax.rem(me + d, count)]]
            push(g, d).start()

        push_edge(g, 0).start()
        push_edge(g, 1).start()
        incoming[g, 0] = blocks[place[me]]

    attend(0)
    pl.semaphore_wait(barrier, count - 1)
    send(0)

    @pl.loop(1, steps)
    def _(g):
        attend(g)
        send(g)

    for load in loads:
        load.wait()
    layer_ref[...] = dot(mixed[...], weights[0], NN).astype(jnp.bfloat16)
    total[...] = dot(query_grad[...], weights[1], NT)

    @pl.loop(0, steps)
    def _(g):
        lanes = pl.ds(pl.multiple_of(g * cols, cols), cols)
        others = pl.ds(1, count - 1)
        pltpu.make_async_copy(incoming.at[g, others], incoming.at[g, others], recv_sem.at[g]).wait()
        push_edge(g, 0).wait_recv()
        push_edge(g, 1).wait_recv()
        for kv in range(2):
            came = incoming[g, :, kv].reshape((count + 2) * tile, cols)
            whole = sums[kv, :, lanes] + dot(pick[...], came, NN)
            total[...] += dot(whole.astype(jnp.bfloat16), weights[2 + kv, :, lanes], NT)

    grad_ref[...] = total[...].astype(jnp.bfloat16)

    @pl.loop(0, steps)
    def _(g):
        others = pl.ds(1, count - 1)
        pltpu.make_async_copy(outgoing.at[g, others], outgoing.at[g, others], send_sem.at[g]).wait()
        push_edge(g, 0).wait_send()
        push_edge(g, 1).wait_send()


def on_device(
    latents, w_query, w_key, w_value, w_out, cotangent, memory_ids, memory_count, tile_mask
):
    frames, tile, width = latents.shape
    count = lax.axis_size("tm")
    me = lax.axis_index("tm")
    rows = latents.reshape(-1, width)
    mem = memory_ids.shape[1]
    inner = w_query.shape[1]
    head_dim = inner // HEADS
    cols = GROUP * head_dim
    steps = inner // cols
    up = [(i, i + 1) for i in range(count - 1)]
    down = [(i + 1, i) for i in range(count - 1)]

    owners = (memory_ids // frames).reshape(-1).astype(jnp.int32)
    local = (memory_ids % frames).reshape(-1).astype(jnp.int32)
    peers = jnp.arange(count, dtype=jnp.int32)
    matched = owners[None, :] == peers[:, None]
    wanted = jnp.where(
        jnp.any(matched, axis=1), jnp.sum(jnp.where(matched, local[None, :], 0), axis=1), -1
    )
    asked = lax.all_to_all(wanted[:, None], "tm", split_axis=0, concat_axis=0, tiled=True)[:, 0]
    frame_ids = jnp.arange(frames, dtype=jnp.int32)
    selector = (asked[:, None] == frame_ids[None, :]).astype(jnp.bfloat16)
    outgoing = jnp.einsum(
        "nf,ftc->ntc", selector, latents, preferred_element_type=jnp.float32
    ).astype(jnp.bfloat16)
    received = lax.all_to_all(outgoing, "tm", split_axis=0, concat_axis=0, tiled=True)
    below_rows = lax.ppermute(latents[frames - 1], "tm", up)
    above_rows = lax.ppermute(latents[0], "tm", down)

    def project(block, weight):
        return jnp.dot(block, weight, preferred_element_type=jnp.float32).astype(jnp.bfloat16)

    ext_rows = jnp.concatenate([below_rows, rows, above_rows], axis=0)
    queries = project(rows, w_query)
    k_ext = project(ext_rows, w_key)
    v_ext = project(ext_rows, w_value)
    out_grad = lax.dot_general(
        cotangent.reshape(-1, width), w_out, NT, preferred_element_type=jnp.float32
    ).astype(jnp.bfloat16)
    far_rows = received.reshape(count * tile, width)
    k_mem = project(far_rows, w_key).reshape(count, tile, inner)
    v_mem = project(far_rows, w_value).reshape(count, tile, inner)

    global_ids = me * frames + frame_ids
    lower = (tile_mask[:, 0] * (global_ids >= 1)).astype(jnp.float32)
    upper = (tile_mask[:, 1] * (global_ids < frames * count - 1)).astype(jnp.float32)
    kept = (jnp.arange(mem, dtype=jnp.int32)[None, :] < memory_count[:, None]).astype(jnp.float32)
    valid = jnp.concatenate(
        [lower[:, None], jnp.ones((frames, 1), jnp.float32), upper[:, None], kept], axis=1
    )
    valid = jnp.repeat(valid, tile, axis=1)

    own = frames * tile
    place = jnp.sum(
        jnp.where(matched, jnp.arange(frames * mem, dtype=jnp.int32)[None, :], 0), axis=1
    ).astype(jnp.int32)
    senders = (me - peers) % count
    ends = jnp.array([0, frames - 1], jnp.int32)
    came_for = jnp.concatenate([jnp.take(asked, senders), ends])
    token = jnp.arange(tile, dtype=jnp.int32)
    target = (came_for[:, None] * tile + token[None, :]).reshape(-1)
    target = jnp.where(jnp.repeat(came_for, tile) >= 0, target, -1)
    pick = (jnp.arange(own, dtype=jnp.int32)[:, None] == target[None, :]).astype(jnp.bfloat16)

    vmem = pl.BlockSpec(memory_space=pltpu.VMEM)
    smem = pl.BlockSpec(memory_space=pltpu.SMEM)
    hbm = pl.BlockSpec(memory_space=pl.ANY)
    block = (2, tile, cols)
    layer_out, latent_grad = pl.pallas_call(
        functools.partial(attend_kernel, count, frames, mem, tile, head_dim, steps),
        in_specs=[smem, smem] + [vmem] * 8 + [hbm] * 4,
        out_specs=[vmem, vmem],
        out_shape=[
            jax.ShapeDtypeStruct((own, width), jnp.bfloat16),
            jax.ShapeDtypeStruct((own, width), jnp.bfloat16),
        ],
        scratch_shapes=[
            pltpu.VMEM((4, width, inner), jnp.bfloat16),
            pltpu.VMEM((own, inner), jnp.bfloat16),
            pltpu.VMEM((own, inner), jnp.bfloat16),
            pltpu.VMEM((2, own, inner), jnp.float32),
            pltpu.VMEM((frames * mem,) + block, jnp.bfloat16),
            pltpu.VMEM((steps, count + 2) + block, jnp.bfloat16),
            pltpu.VMEM((steps, count + 2) + block, jnp.bfloat16),
            pltpu.VMEM((own, width), jnp.float32),
            pltpu.SemaphoreType.DMA((4,)),
            pltpu.SemaphoreType.DMA((steps,)),
            pltpu.SemaphoreType.DMA((steps,)),
            pltpu.SemaphoreType.DMA((steps, 2)),
            pltpu.SemaphoreType.DMA((steps, 2)),
        ],
        compiler_params=pltpu.CompilerParams(
            collective_id=0, has_side_effects=True, vmem_limit_bytes=56 * 2**20
        ),
    )(
        owners, place, valid, pick, queries, out_grad, k_ext, v_ext, k_mem, v_mem,
        w_out, w_query, w_key, w_value,
    )
    return (
        layer_out.reshape(frames, tile, width),
        latent_grad.reshape(frames, tile, width),
    )


def solution(mesh):
    placed = (
        P(("shard", "tm"), None, None),
        P(),
        P(),
        P(),
        P(),
        P(("shard", "tm"), None, None),
        P(("shard", "tm"), None),
        P(("shard", "tm")),
        P(("shard", "tm"), None),
    )
    return jax.shard_map(
        on_device,
        mesh=mesh,
        in_specs=placed,
        out_specs=(P(("shard", "tm"), None, None), P(("shard", "tm"), None, None)),
        check_vma=False,
    )
```

time: 196 us -> 158 us (0.81)
  waiting for transfers between devices: 84.7 us -> 16.7 us
  Pallas kernels: 27.9 us -> 79.5 us
  blocking collectives: 10.1 us -> 0 us
  local copies, waits for them, and re-layouts: 16.8 us -> 9.12 us
  starting transfers between devices: 22.3 us -> 17.9 us
  other arithmetic: 1.51 us -> 4.47 us
    ppermute x2 -> x0, waiting for transfers between devices: 61.4 us -> none  [the longest x1 60.3 us: on_device(): from_above = lax.ppermute(edges[0], 'tm', down)]
    pallas_call x2 -> x1, Pallas kernels: 27.9 us -> 79.5 us  [on_device(): pl.pallas_call(functools.partial(attend_kernel, count, frames, mem, tile,...]
    ppermute x1, waiting for transfers between devices: 23.3 us -> 0.01 us  [on_device(): below_rows = lax.ppermute(latents[frames - 1], 'tm', up)]
    all_to_all x1, waiting for transfers between devices: 0.01 us -> 16.7 us  [on_device(): lax.all_to_all(outgoing, 'tm', split_axis=0, concat_axis=0, tiled=True)]
    all_to_all x1 -> x0, blocking collectives: 10.1 us -> none  [on_device(): lax.all_to_all(wanted[:, None], 'tm', split_axis=0, concat_axis=0, tiled=...]
    unnamed x32 -> x12, local copies, waits for them, and re-layouts: 13 us -> 3.56 us
    ppermute x2 -> x0, starting transfers between devices: 5.04 us -> none  [the longest x1 3.12 us: on_device(): from_above = lax.ppermute(edges[0], 'tm', down)]
    dot_general x6 -> x5, matrix products: 24.8 us -> 22.3 us  [project(): jnp.dot(block, weight, preferred_element_type=jnp.float32)]
  transfers between devices with their start and end apart: 6 -> 4, of which waited for: 3 -> 1; matrix products, arithmetic and copies ran while one was open for 10% -> 17% of each run, Pallas kernels for 0% -> 0%
where the time goes in v1:
time: 158 us; the launch traced here: 157 us
  Pallas kernels  79.5 us (50%)
  matrix products  28.7 us (18%)
  starting transfers between devices  17.9 us (11%)
  waiting for transfers between devices  16.7 us (11%)
  local copies, waits for them, and re-layouts  9.12 us (6%)
  other arithmetic  4.47 us (3%)
    pallas_call x1, Pallas kernels, on_device(): pl.pallas_call(functools.partial(attend_kernel, count, frames, mem, tile,...  79.5 us
    dot_general x5, matrix products, project(): jnp.dot(block, weight, preferred_element_type=jnp.float32)  22.3 us
    all_to_all x1, waiting for transfers between devices, on_device(): lax.all_to_all(outgoing, 'tm', split_axis=0, concat_axis=0, tiled=True)  16.7 us
    all_to_all x1, starting transfers between devices, on_device(): lax.all_to_all(wanted[:, None], 'tm', split_axis=0, concat_axis=0, tiled=...  6.18 us
    all_to_all x1, starting transfers between devices, on_device(): lax.all_to_all(outgoing, 'tm', split_axis=0, concat_axis=0, tiled=True)  5.25 us
    dot_general x1, matrix products, on_device(): lax.dot_general(cotangent.reshape(-1, width), w_out, NT, preferred_elemen...  4.7 us
    ppermute x1, starting transfers between devices, on_device(): above_rows = lax.ppermute(latents[0], 'tm', down)  4.4 us
    unnamed x12, local copies, waits for them, and re-layouts  3.56 us
  transfers between devices with their start and end apart: 4, of which 1 were waited for; matrix products, arithmetic and copies ran while one was open for 17% of the time, Pallas kernels for 0%

profile of v1, /device:TPU:16, one launch (start us, length us, event | category | flops | bytes accessed | tf_op | source)
XLA Modules:
  0.0 157.2 jit_solution(4599224171866427681)
XLA Ops:
  0.6 0.7 add_select_fusion.1
  1.7 0.7 select_reduce_fusion
  2.4 0.7 copy.31
  3.1 6.2 %all-to-all-start = ((s32[16,1,1]{2,1,0:T(1,128)}), s32[16,1,1]{2,1,0:T(1,128)S(1)}, u32[]{:S(2)}, u32[]{:S(2)}) async-start(s32[16,1,1]{2,1,0:T(1,128)} %copy.31), calls=%async_computation | async-start | bytes 16384 | tf_op jit(solution)/shard_map/all_to_all | solution.py:204
  9.2 1.0 slice_bitcast_fusion.1
  10.2 2.1 %collective-permute-start = (bf16[32,1536]{1,0:T(8,128)(2,1)S(1)}, bf16[32,1536]{1,0:T(8,128)(2,1)S(1)}, u32[]{:S(2)}, u32[]{:S(2)}) collective-permute-start(bf16[32,1536]{1,0:T(8,128)(2,1)S(1)} %get-tuple-element.8), channel_id=1, source_target_pairs={{0,1},{1,2},{2,3},{3,4},{4,5},{5,6},{6,7},{7,8},{8,9},{9,10},{10,1... | collective-permute-start | bytes 294920 | tf_op jit(solution)/shard_map/ppermute | solution.py:211
  12.3 4.4 %collective-permute-start.1 = (bf16[32,1536]{1,0:T(8,128)(2,1)S(1)}, bf16[32,1536]{1,0:T(8,128)(2,1)S(1)}, u32[]{:S(2)}, u32[]{:S(2)}) collective-permute-start(bf16[32,1536]{1,0:T(8,128)(2,1)S(1)} %get-tuple-element.9), channel_id=1, source_target_pairs={{1,0},{2,1},{3,2},{4,3},{5,4},{6,5},{7,6},{8,7},{9,8},{10,9},{11,1... | collective-permute-start | bytes 294920 | tf_op jit(solution)/shard_map/ppermute | solution.py:212
  16.7 0.8 fusion.8
  17.6 0.7 fusion.4
  18.8 1.7 %convolution_convert_fusion.2 = bf16[16,32,1536]{2,0,1:T(8,128)(2,1)S(1)} fusion(bf16[4,32,1536]{2,1,0:T(8,128)(2,1)} %param.10, s32[16]{0:T(128)S(1)} %reduce), kind=kOutput, calls=%fused_computation.3 | convolution fusion | flops 7077952 | bytes 1966144 | tf_op jit(solution)/shard_map/nf,ftc->ntc/dot_general | solution.py:207
  20.5 2.0 %copy.33 = bf16[16,32,1536]{2,1,0:T(8,128)(2,1)} copy(bf16[16,32,1536]{2,0,1:T(8,128)(2,1)S(1)} %convolution_convert_fusion.2) | data formatting | bytes 3145728 | tf_op jit(solution)/shard_map/convert_element_type | solution.py:209
  22.5 5.3 %all-to-all-start.1 = ((bf16[16,32,1536]{2,1,0:T(8,128)(2,1)}), bf16[16,32,1536]{2,1,0:T(8,128)(2,1)S(1)}, u32[]{:S(2)}, u32[]{:S(2)}) async-start(bf16[16,32,1536]{2,1,0:T(8,128)(2,1)} %copy.33), calls=%async_computation.1 | async-start | bytes 3145728 | tf_op jit(solution)/shard_map/all_to_all | solution.py:210
  27.9 0.7 reshape.162.valid
  28.6 3.9 %convolution_convert_fusion.6.q_ref = bf16[128,1536]{1,0:T(8,128)(2,1)} fusion(bf16[128,1536]{1,0:T(8,128)(2,1)S(1)} %bitcast.32, bf16[1536,1536]{1,0:T(8,128)(2,1)} %wq_hbm.1), kind=kOutput, calls=%fused_computation.7 | convolution fusion | flops 604176384 | bytes 5505024 | tf_op jit(solution)/shard_map/dot_general | solution.py:215
  32.5 4.7 %convolution_convert_fusion.5.g_ref = bf16[128,1536]{1,0:T(8,128)(2,1)} fusion(bf16[128,1536]{1,0:T(8,128)(2,1)S(1)} %bitcast.29, bf16[1536,1536]{1,0:T(8,128)(2,1)} %wo_hbm.1), kind=kOutput, calls=%fused_computation.6 | convolution fusion | flops 604176384 | bytes 5505024 | tf_op jit(solution)/shard_map/dot_general | solution.py:221
  38.2 0.7 fusion.1.pick
  38.9 4.2 %convolution_convert_fusion.3.v_ext = bf16[192,1536]{1,0:T(8,128)(2,1)} fusion(bf16[1536,1536]{1,0:T(8,128)(2,1)} %wv_hbm.1, bf16[32,1536]{1,0:T(8,128)(2,1)S(1)} %collective-permute-done.1, bf16[128,1536]{1,0:T(8,128)(2,1)S(1)} %bitcast.33, bf16[32,1536]{1,0:T(8,128)(2,1)S(1)} %collective-permute-done), kind=kOutput, calls=%fused_computation.4 | convolution fusion | flops 908034048 | bytes 5898240 | tf_op jit(solution)/shard_map/dot_general | solution.py:215
  43.2 4.3 %convolution_convert_fusion.4.k_ext = bf16[192,1536]{1,0:T(8,128)(2,1)} fusion(bf16[1536,1536]{1,0:T(8,128)(2,1)} %wk_hbm.1, bf16[32,1536]{1,0:T(8,128)(2,1)S(1)} %collective-permute-done.1, bf16[128,1536]{1,0:T(8,128)(2,1)S(1)} %bitcast.34, bf16[32,1536]{1,0:T(8,128)(2,1)S(1)} %collective-permute-done), kind=kOutput, calls=%fused_computation.5 | convolution fusion | flops 908034048 | bytes 5898240 | tf_op jit(solution)/shard_map/dot_general | solution.py:215
  47.5 16.7 %all-to-all-done.1 = bf16[16,32,1536]{2,1,0:T(8,128)(2,1)S(1)} async-done(((bf16[16,32,1536]{2,1,0:T(8,128)(2,1)}), bf16[16,32,1536]{2,1,0:T(8,128)(2,1)S(1)}, u32[]{:S(2)}, u32[]{:S(2)}) %all-to-all-start.1) | async-done | bytes 1572896 | tf_op jit(solution)/shard_map/all_to_all | solution.py:210
  64.2 6.2 %convolution_convert_fusion.1 = bf16[512,1536]{1,0:T(8,128)(2,1)} fusion(bf16[512,1536]{1,0:T(8,128)(2,1)S(1)} %bitcast.37, bf16[1536,1536]{1,0:T(8,128)(2,1)} %wk_hbm.1), kind=kOutput, calls=%fused_computation.2 | convolution fusion | flops 2416705536 | bytes 7864320 | tf_op jit(solution)/shard_map/dot_general | solution.py:215
  70.3 3.7 %convolution_convert_fusion = bf16[512,1536]{1,0:T(8,128)(2,1)} fusion(bf16[512,1536]{1,0:T(8,128)(2,1)S(1)} %bitcast.38, bf16[1536,1536]{1,0:T(8,128)(2,1)S(1)} %bitcast.31), kind=kOutput, calls=%fused_computation.1 | convolution fusion | flops 2416705536 | bytes 7864320 | tf_op jit(solution)/shard_map/dot_general | solution.py:215
  74.1 79.5 %shard_map.113 = (bf16[128,1536]{1,0:T(8,128)(2,1)}, bf16[128,1536]{1,0:T(8,128)(2,1)}) custom-call(s32[16]{0:T(128)} %copy-done.2, s32[16]{0:T(128)} %get-tuple-element.7.place, f32[4,224]{1,0:T(4,128)} %reshape.162.valid, bf16[128,576]{1,0:T(8,128)(2,1)} %fusion.1.pick, bf16[128,1536]{1,0:T(8,128)(2,1)} %convolution_convert_fusion.6.q_ref, ...), custom_call_target="tpu_custom_call" | custom-call | tf_op jit(solution)/shard_map/pallas_call | solution.py:253
  153.6 1.8 %copy.38 = bf16[4,32,1536]{2,1,0:T(8,128)(2,1)} copy(bf16[4,32,1536]{2,1,0:T(8,128)(2,1)} %bitcast.40) | data formatting | bytes 786432
  155.4 1.8 %copy.39 = bf16[4,32,1536]{2,1,0:T(8,128)(2,1)} copy(bf16[4,32,1536]{2,1,0:T(8,128)(2,1)} %bitcast.39) | data formatting | bytes 786432
  (33 shorter events, 2.1 us)
Async XLA Ops:
  0.6 31.9 %copy-start = (bf16[4,32,1536]{2,1,0:T(8,128)(2,1)S(1)}, bf16[4,32,1536]{2,1,0:T(8,128)(2,1)}, u32[]{:S(2)}) copy-start(bf16[4,32,1536]{2,1,0:T(8,128)(2,1)} %param.15) | copy-start | bytes 1179652
  1.5 21.0 %copy-start.2 = (s32[16]{0:T(128)}, s32[16]{0:T(128)S(1)}, u32[]{:S(2)}) copy-start(s32[16]{0:T(128)S(1)} %reshape.161.owners) | copy-start | bytes 196
  3.1 15.4 %all-to-all-start = ((s32[16,1,1]{2,1,0:T(1,128)}), s32[16,1,1]{2,1,0:T(1,128)S(1)}, u32[]{:S(2)}, u32[]{:S(2)}) async-start(s32[16,1,1]{2,1,0:T(1,128)} %copy.31), calls=%async_computation | async-start | bytes 16384 | tf_op jit(solution)/shard_map/all_to_all | solution.py:204
  10.2 28.7 %collective-permute-start = (bf16[32,1536]{1,0:T(8,128)(2,1)S(1)}, bf16[32,1536]{1,0:T(8,128)(2,1)S(1)}, u32[]{:S(2)}, u32[]{:S(2)}) collective-permute-start(bf16[32,1536]{1,0:T(8,128)(2,1)S(1)} %get-tuple-element.8), channel_id=1, source_target_pairs={{0,1},{1,2},{2,3},{3,4},{4,5},{5,6},{6,7},{7,8},{8,9},{9,10},{10,1... | collective-permute-start | bytes 294920 | tf_op jit(solution)/shard_map/ppermute | solution.py:211
  12.3 26.6 %collective-permute-start.1 = (bf16[32,1536]{1,0:T(8,128)(2,1)S(1)}, bf16[32,1536]{1,0:T(8,128)(2,1)S(1)}, u32[]{:S(2)}, u32[]{:S(2)}) collective-permute-start(bf16[32,1536]{1,0:T(8,128)(2,1)S(1)} %get-tuple-element.9), channel_id=1, source_target_pairs={{1,0},{2,1},{3,2},{4,3},{5,4},{6,5},{7,6},{8,7},{9,8},{10,9},{11,1... | collective-permute-start | bytes 294920 | tf_op jit(solution)/shard_map/ppermute | solution.py:212
  22.5 6.1 %copy-start.1 = (bf16[4,32,1536]{2,1,0:T(8,128)(2,1)S(1)}, bf16[4,32,1536]{2,1,0:T(8,128)(2,1)}, u32[]{:S(2)}) copy-start(bf16[4,32,1536]{2,1,0:T(8,128)(2,1)} %param.10) | copy-start | bytes 1179652
  22.5 41.7 %all-to-all-start.1 = ((bf16[16,32,1536]{2,1,0:T(8,128)(2,1)}), bf16[16,32,1536]{2,1,0:T(8,128)(2,1)S(1)}, u32[]{:S(2)}, u32[]{:S(2)}) async-start(bf16[16,32,1536]{2,1,0:T(8,128)(2,1)} %copy.33), calls=%async_computation.1 | async-start | bytes 3145728 | tf_op jit(solution)/shard_map/all_to_all | solution.py:210
  43.2 27.2 %slice-start = ((s8[4718592]{0:T(1024)(128)(4,1)}), s8[524288]{0:T(1024)(128)(4,1)S(1)}, s32[]{:S(2)}) async-start(s8[4718592]{0:T(1024)(128)(4,1)} %bitcast.30), calls=%async_computation.2 | async-start | bytes 1048576
  64.2 6.2 %slice-start.1 = ((s8[4718592]{0:T(1024)(128)(4,1)}), s8[4194304]{0:T(1024)(128)(4,1)S(1)}, s32[]{:S(2)}) async-start(s8[4718592]{0:T(1024)(128)(4,1)} %bitcast.30), calls=%async_computation.3 | async-start | bytes 8388608

commit v2 on v1

--- a/solution.py
+++ b/solution.py
@@ -20,33 +20,172 @@
     return lax.dot_general(a, b, dims, preferred_element_type=jnp.float32)
 
 
-def attend_kernel(
+CHUNK = 8
+
+
+def layer_kernel(
     count, frames, mem, tile, head_dim, steps,
-    owners, place, valid, pick, q_ref, g_ref, k_ext, v_ext, k_mem, v_mem,
-    wo_hbm, wq_hbm, wk_hbm, wv_hbm,
+    spots, place, valid, x_ref, cot_ref, want_out,
+    wq_hbm, wo_hbm, wk_hbm, wv_hbm,
     layer_ref, grad_ref,
-    weights, mixed, query_grad, sums, blocks, outgoing, incoming, total,
-    weight_sem, send_sem, recv_sem, edge_send, edge_recv,
+    weights, q_ref, g_ref, k_ext, v_ext, k_mem, v_mem, want_in, choose, rows_out, rows_in,
+    mixed, query_grad, sums, blocks, outgoing, incoming, total,
+    weight_sem, want_send, want_recv, row_send, row_recv, halo_send, halo_recv,
+    send_sem, recv_sem, edge_send, edge_recv,
 ):
     me = lax.axis_index("tm")
     width = q_ref.shape[1]
+    own = q_ref.shape[0]
     cols = width // steps
+    wide = 2 * cols
     rows = GROUP * tile
     inv_root = 1.0 / math.sqrt(head_dim)
     loads = [
         pltpu.make_async_copy(source, weights.at[i], weight_sem.at[i])
-        for i, source in enumerate((wo_hbm, wq_hbm, wk_hbm, wv_hbm))
+        for i, source in enumerate((wq_hbm, wo_hbm, wk_hbm, wv_hbm))
     ]
     for load in loads:
         load.start()
 
+    def shift(i):
+        half = i // 2
+        return count // 2 + (i % 2) * 2 * half - half
+
+    def peer(i):
+        return {"tm": lax.rem(me + shift(i), count)}
+
+    def asker(i):
+        return {"tm": lax.rem(me + count - shift(i), count)}
+
+    def beside(side):
+        return {"tm": lax.rem(me + (1 if side == 0 else count - 1), count)}
+
     barrier = pltpu.get_barrier_semaphore()
 
     @pl.loop(1, count)
-    def _(d):
-        pl.semaphore_signal(
-            barrier, inc=1, device_id={"tm": lax.rem(me + d, count)}, device_id_type=MESH
+    def _(i):
+        pl.semaphore_signal(barrier, inc=1, device_id=peer(i), device_id_type=MESH)
+
+    pl.semaphore_wait(barrier, count - 1)
+
+    def ask(i):
+        return pltpu.make_async_remote_copy(
+            src_ref=want_out.at[i], dst_ref=want_in.at[i], send_sem=want_send,
+            recv_sem=want_recv, device_id=peer(i), device_id_type=MESH,
         )
+
+    def push_halo(side):
+        return pltpu.make_async_remote_copy(
+            src_ref=x_ref.at[pl.ds((frames - 1) * tile if side == 0 else 0, tile)],
+            dst_ref=rows_in.at[count + side],
+            send_sem=halo_send.at[side], recv_sem=halo_recv.at[side],
+            device_id=beside(side), device_id_type=MESH,
+        )
+
+    def push_row(i, c):
+        return pltpu.make_async_remote_copy(
+            src_ref=rows_out.at[i], dst_ref=rows_in.at[i], send_sem=row_send,
+            recv_sem=row_recv.at[c], device_id=asker(i), device_id_type=MESH,
+        )
+
+    @pl.loop(1, count)
+    def _(i):
+        ask(i).start()
+
+    push_halo(0).start()
+    push_halo(1).start()
+    want_in[0] = want_out[0]
+    others = pl.ds(1, count - 1)
+    pltpu.make_async_copy(want_in.at[others], want_in.at[others], want_recv).wait()
+
+    chunks = count // CHUNK
+    shape = (CHUNK, tile, own)
+    token = lax.broadcasted_iota(jnp.int32, shape, 1)
+    lane = lax.broadcasted_iota(jnp.int32, shape, 2)
+
+    def pick_rows(c):
+        asked = want_in[pl.ds(c * CHUNK, CHUNK)][:, 0:1, :]
+        hot = jnp.where(lane == asked * tile + token, 1.0, 0.0).astype(jnp.bfloat16)
+        hot = hot.reshape(CHUNK * tile, own)
+        choose[pl.ds(pl.multiple_of(c * (CHUNK * tile), CHUNK * tile), CHUNK * tile), :] = hot
+        for part in range(width // wide):
+            lanes = slice(part * wide, (part + 1) * wide)
+            rows_out[pl.ds(c * CHUNK, CHUNK), :, lanes] = (
+                dot(hot, x_ref[:, lanes], NN).astype(jnp.bfloat16).reshape(CHUNK, tile, wide)
+            )
+
+    pick_rows(0)
+
+    @pl.loop(1, CHUNK)
+    def _(i):
+        push_row(i, 0).start()
+
+    rows_in[0] = rows_out[0]
+
+    @pl.loop(1, chunks)
+    def _(c):
+        pick_rows(c)
+
+        @pl.loop(0, CHUNK)
+        def _(i):
+            push_row(c * CHUNK + i, c).start()
+
+    edge_row = lax.broadcasted_iota(jnp.int32, (2 * tile, own), 0)
+    edge_lane = lax.broadcasted_iota(jnp.int32, (2 * tile, own), 1)
+    edge_spot = jnp.where(edge_row < tile, edge_row, edge_row + (frames - 2) * tile)
+    choose[count * tile : (count + 2) * tile, :] = jnp.where(
+        edge_lane == edge_spot, 1.0, 0.0
+    ).astype(jnp.bfloat16)
+
+    loads[0].wait()
+
+    @pl.loop(0, width // wide)
+    def _(p):
+        lanes = pl.ds(pl.multiple_of(p * wide, wide), wide)
+        q_ref[:, lanes] = dot(x_ref[...], weights[0, :, lanes], NN).astype(jnp.bfloat16)
+
+    loads[1].wait()
+
+    @pl.loop(0, width // wide)
+    def _(p):
+        lanes = pl.ds(pl.multiple_of(p * wide, wide), wide)
+        g_ref[:, lanes] = dot(cot_ref[...], weights[1, lanes, :], NT).astype(jnp.bfloat16)
+
+    push_halo(0).wait_recv()
+    push_halo(1).wait_recv()
+    loads[2].wait()
+    loads[3].wait()
+
+    @pl.loop(0, width // wide)
+    def _(p):
+        lanes = pl.ds(pl.multiple_of(p * wide, wide), wide)
+        ext = jnp.concatenate([rows_in[count], x_ref[...], rows_in[count + 1]], axis=0)
+        k_ext[:, lanes] = dot(ext, weights[2, :, lanes], NN).astype(jnp.bfloat16)
+        v_ext[:, lanes] = dot(ext, weights[3, :, lanes], NN).astype(jnp.bfloat16)
+
+    def project(c):
+        some = pl.ds(c * CHUNK, CHUNK)
+
+        @pl.loop(0, width // wide)
+        def _(p):
+            lanes = pl.ds(pl.multiple_of(p * wide, wide), wide)
+            flat = rows_in[some].reshape(CHUNK * tile, width)
+            for weight, far in ((2, k_mem), (3, v_mem)):
+                far[some, :, lanes] = (
+                    dot(flat, weights[weight, :, lanes], NN)
+                    .astype(jnp.bfloat16)
+                    .reshape(CHUNK, tile, wide)
+                )
+
+    first = pl.ds(1, CHUNK - 1)
+    pltpu.make_async_copy(rows_in.at[first], rows_in.at[first], row_recv.at[0]).wait()
+    project(0)
+
+    @pl.loop(1, chunks)
+    def _(c):
+        some = pl.ds(c * CHUNK, CHUNK)
+        pltpu.make_async_copy(rows_in.at[some], rows_in.at[some], row_recv.at[c]).wait()
+        project(c)
 
     own_head = (
         lax.broadcasted_iota(jnp.int32, (rows, cols), 0) // tile
@@ -70,7 +209,7 @@
             dst_ref=incoming.at[g, d],
             send_sem=send_sem.at[g],
             recv_sem=recv_sem.at[g],
-            device_id={"tm": lax.rem(me + d, count)},
+            device_id=peer(d),
             device_id_type=MESH,
         )
 
@@ -80,7 +219,7 @@
             dst_ref=incoming.at[g, count + side],
             send_sem=edge_send.at[g, side],
             recv_sem=edge_recv.at[g, side],
-            device_id={"tm": lax.rem(me + (1 if side == 0 else count - 1), count)},
+            device_id=beside(side),
             device_id_type=MESH,
         )
 
@@ -92,7 +231,7 @@
 
             def gather(ext, far):
                 return jnp.concatenate(
-                    [ext[near, lanes]] + [far[owners[f * mem + j], :, lanes] for j in range(mem)],
+                    [ext[near, lanes]] + [far[spots[f * mem + j], :, lanes] for j in range(mem)],
                     axis=0,
                 )
 
@@ -136,44 +275,42 @@
     def send(g):
         @pl.loop(1, count)
         def _(d):
-            outgoing[g, d] = blocks[place[lax.rem(me + d, count)]]
+            outgoing[g, d] = blocks[place[d]]
             push(g, d).start()
 
         push_edge(g, 0).start()
         push_edge(g, 1).start()
-        incoming[g, 0] = blocks[place[me]]
-
-    attend(0)
-    pl.semaphore_wait(barrier, count - 1)
-    send(0)
-
-    @pl.loop(1, steps)
+        incoming[g, 0] = blocks[place[0]]
+
+    @pl.loop(0, steps)
     def _(g):
         attend(g)
         send(g)
 
-    for load in loads:
-        load.wait()
-    layer_ref[...] = dot(mixed[...], weights[0], NN).astype(jnp.bfloat16)
-    total[...] = dot(query_grad[...], weights[1], NT)
+    for part in range(width // wide):
+        lanes = slice(part * wide, (part + 1) * wide)
+        layer_ref[:, lanes] = dot(mixed[...], weights[1, :, lanes], NN).astype(jnp.bfloat16)
+        total[:, lanes] = dot(query_grad[...], weights[0, lanes, :], NT)
 
     @pl.loop(0, steps)
     def _(g):
         lanes = pl.ds(pl.multiple_of(g * cols, cols), cols)
-        others = pl.ds(1, count - 1)
         pltpu.make_async_copy(incoming.at[g, others], incoming.at[g, others], recv_sem.at[g]).wait()
         push_edge(g, 0).wait_recv()
         push_edge(g, 1).wait_recv()
         for kv in range(2):
             came = incoming[g, :, kv].reshape((count + 2) * tile, cols)
-            whole = sums[kv, :, lanes] + dot(pick[...], came, NN)
+            whole = sums[kv, :, lanes] + dot(choose[...], came, TN)
             total[...] += dot(whole.astype(jnp.bfloat16), weights[2 + kv, :, lanes], NT)
 
     grad_ref[...] = total[...].astype(jnp.bfloat16)
+    pltpu.make_async_copy(want_out.at[others], want_out.at[others], want_send).wait()
+    pltpu.make_async_copy(rows_out.at[others], rows_out.at[others], row_send).wait()
+    push_halo(0).wait_send()
+    push_halo(1).wait_send()
 
     @pl.loop(0, steps)
     def _(g):
-        others = pl.ds(1, count - 1)
         pltpu.make_async_copy(outgoing.at[g, others], outgoing.at[g, others], send_sem.at[g]).wait()
         push_edge(g, 0).wait_send()
         push_edge(g, 1).wait_send()
@@ -191,39 +328,24 @@
     head_dim = inner // HEADS
     cols = GROUP * head_dim
     steps = inner // cols
-    up = [(i, i + 1) for i in range(count - 1)]
-    down = [(i + 1, i) for i in range(count - 1)]
-
-    owners = (memory_ids // frames).reshape(-1).astype(jnp.int32)
-    local = (memory_ids % frames).reshape(-1).astype(jnp.int32)
-    peers = jnp.arange(count, dtype=jnp.int32)
-    matched = owners[None, :] == peers[:, None]
-    wanted = jnp.where(
-        jnp.any(matched, axis=1), jnp.sum(jnp.where(matched, local[None, :], 0), axis=1), -1
-    )
-    asked = lax.all_to_all(wanted[:, None], "tm", split_axis=0, concat_axis=0, tiled=True)[:, 0]
+    order = jnp.arange(count, dtype=jnp.int32)
+    half = order // 2
+    shift = jnp.where(order == 0, 0, count // 2 + jnp.where(order % 2 == 1, half, -half))
+    targets = (me + shift) % count
+
+    owners = (memory_ids // frames).reshape(1, -1).astype(jnp.int32)
+    local = (memory_ids % frames).reshape(1, -1).astype(jnp.int32)
+    entry = jnp.arange(frames * mem, dtype=jnp.int32)
+    spots = jnp.sum(jnp.where(targets[:, None] == owners, order[:, None], 0), axis=0)
+    spots = spots.astype(jnp.int32)
+    matched = targets[:, None] == owners
+    place = jnp.sum(jnp.where(matched, entry[None, :], 0), axis=1).astype(jnp.int32)
+    wanted = jnp.sum(jnp.where(matched, local + 1, 0), axis=1).astype(jnp.int32) - 1
+    own = frames * tile
+    want_out = jnp.broadcast_to(
+        jnp.where(wanted < 0, -frames, wanted)[:, None, None], (count, 8, own)
+    )
     frame_ids = jnp.arange(frames, dtype=jnp.int32)
-    selector = (asked[:, None] == frame_ids[None, :]).astype(jnp.bfloat16)
-    outgoing = jnp.einsum(
-        "nf,ftc->ntc", selector, latents, preferred_element_type=jnp.float32
-    ).astype(jnp.bfloat16)
-    received = lax.all_to_all(outgoing, "tm", split_axis=0, concat_axis=0, tiled=True)
-    below_rows = lax.ppermute(latents[frames - 1], "tm", up)
-    above_rows = lax.ppermute(latents[0], "tm", down)
-
-    def project(block, weight):
-        return jnp.dot(block, weight, preferred_element_type=jnp.float32).astype(jnp.bfloat16)
-
-    ext_rows = jnp.concatenate([below_rows, rows, above_rows], axis=0)
-    queries = project(rows, w_query)
-    k_ext = project(ext_rows, w_key)
-    v_ext = project(ext_rows, w_value)
-    out_grad = lax.dot_general(
-        cotangent.reshape(-1, width), w_out, NT, preferred_element_type=jnp.float32
-    ).astype(jnp.bfloat16)
-    far_rows = received.reshape(count * tile, width)
-    k_mem = project(far_rows, w_key).reshape(count, tile, inner)
-    v_mem = project(far_rows, w_value).reshape(count, tile, inner)
 
     global_ids = me * frames + frame_ids
     lower = (tile_mask[:, 0] * (global_ids >= 1)).astype(jnp.float32)
@@ -234,25 +356,13 @@
     )
     valid = jnp.repeat(valid, tile, axis=1)
 
-    own = frames * tile
-    place = jnp.sum(
-        jnp.where(matched, jnp.arange(frames * mem, dtype=jnp.int32)[None, :], 0), axis=1
-    ).astype(jnp.int32)
-    senders = (me - peers) % count
-    ends = jnp.array([0, frames - 1], jnp.int32)
-    came_for = jnp.concatenate([jnp.take(asked, senders), ends])
-    token = jnp.arange(tile, dtype=jnp.int32)
-    target = (came_for[:, None] * tile + token[None, :]).reshape(-1)
-    target = jnp.where(jnp.repeat(came_for, tile) >= 0, target, -1)
-    pick = (jnp.arange(own, dtype=jnp.int32)[:, None] == target[None, :]).astype(jnp.bfloat16)
-
     vmem = pl.BlockSpec(memory_space=pltpu.VMEM)
     smem = pl.BlockSpec(memory_space=pltpu.SMEM)
     hbm = pl.BlockSpec(memory_space=pl.ANY)
     block = (2, tile, cols)
     layer_out, latent_grad = pl.pallas_call(
-        functools.partial(attend_kernel, count, frames, mem, tile, head_dim, steps),
-        in_specs=[smem, smem] + [vmem] * 8 + [hbm] * 4,
+        functools.partial(layer_kernel, count, frames, mem, tile, head_dim, steps),
+        in_specs=[smem, smem] + [vmem] * 4 + [hbm] * 4,
         out_specs=[vmem, vmem],
         out_shape=[
             jax.ShapeDtypeStruct((own, width), jnp.bfloat16),
@@ -262,23 +372,39 @@
             pltpu.VMEM((4, width, inner), jnp.bfloat16),
             pltpu.VMEM((own, inner), jnp.bfloat16),
             pltpu.VMEM((own, inner), jnp.bfloat16),
+            pltpu.VMEM((own + 2 * tile, inner), jnp.bfloat16),
+            pltpu.VMEM((own + 2 * tile, inner), jnp.bfloat16),
+            pltpu.VMEM((count, tile, inner), jnp.bfloat16),
+            pltpu.VMEM((count, tile, inner), jnp.bfloat16),
+            pltpu.VMEM((count, 8, own), jnp.int32),
+            pltpu.VMEM(((count + 2) * tile, own), jnp.bfloat16),
+            pltpu.VMEM((count, tile, width), jnp.bfloat16),
+            pltpu.VMEM((count + 2, tile, width), jnp.bfloat16),
+            pltpu.VMEM((own, inner), jnp.bfloat16),
+            pltpu.VMEM((own, inner), jnp.bfloat16),
             pltpu.VMEM((2, own, inner), jnp.float32),
             pltpu.VMEM((frames * mem,) + block, jnp.bfloat16),
             pltpu.VMEM((steps, count + 2) + block, jnp.bfloat16),
             pltpu.VMEM((steps, count + 2) + block, jnp.bfloat16),
             pltpu.VMEM((own, width), jnp.float32),
             pltpu.SemaphoreType.DMA((4,)),
+            pltpu.SemaphoreType.DMA,
+            pltpu.SemaphoreType.DMA,
+            pltpu.SemaphoreType.DMA,
+            pltpu.SemaphoreType.DMA((count // CHUNK,)),
+            pltpu.SemaphoreType.DMA((2,)),
+            pltpu.SemaphoreType.DMA((2,)),
             pltpu.SemaphoreType.DMA((steps,)),
             pltpu.SemaphoreType.DMA((steps,)),
             pltpu.SemaphoreType.DMA((steps, 2)),
             pltpu.SemaphoreType.DMA((steps, 2)),
         ],
         compiler_params=pltpu.CompilerParams(
-            collective_id=0, has_side_effects=True, vmem_limit_bytes=56 * 2**20
+            collective_id=0, has_side_effects=True, vmem_limit_bytes=58 * 2**20
         ),
     )(
-        owners, place, valid, pick, queries, out_grad, k_ext, v_ext, k_mem, v_mem,
-        w_out, w_query, w_key, w_value,
+        spots, place, valid, rows, cotangent.reshape(-1, width), want_out,
+        w_query, w_out, w_key, w_value,
     )
     return (
         layer_out.reshape(frames, tile, width),

time: 158 us -> 129 us (0.82)
  Pallas kernels: 79.5 us -> 120 us
  matrix products: 28.7 us -> 0 us
  starting transfers between devices: 17.9 us -> 0 us
  waiting for transfers between devices: 16.7 us -> 0 us
  local copies, waits for them, and re-layouts: 9.12 us -> 5.42 us
    pallas_call x1, Pallas kernels: 79.5 us -> 120 us  [on_device(): pl.pallas_call(functools.partial(layer_kernel, count, frames, mem, tile,...]
    dot_general x7 -> x0, matrix products: 28.7 us -> none  [the longest x5 22.3 us: project(): jnp.dot(block, weight, preferred_element_type=jnp.float32)]
    all_to_all x2 -> x0, waiting for transfers between devices: 16.7 us -> none  [the longest x1 16.7 us: on_device(): lax.all_to_all(outgoing, 'tm', split_axis=0, concat_axis=0, tiled=True)]
    all_to_all x2 -> x0, starting transfers between devices: 11.4 us -> none  [the longest x1 6.18 us: on_device(): lax.all_to_all(wanted[:, None], 'tm', split_axis=0, concat_axis=0, tiled=...]
    ppermute x2 -> x0, starting transfers between devices: 6.46 us -> none  [the longest x1 4.4 us: on_device(): above_rows = lax.ppermute(latents[0], 'tm', down)]
    convert_element_type x1 -> x0, local copies, waits for them, and re-layouts: 2.02 us -> none  [on_device(): outgoing = jnp.einsum('nf,ftc->ntc', selector, latents, preferred_element...]
    unnamed x12 -> x2, local copies, waits for them, and re-layouts: 3.56 us -> 3.53 us
  transfers between devices with their start and end apart: 4 -> 0, of which waited for: 1 -> 0; matrix products, arithmetic and copies ran while one was open for 17% -> 0% of each run, Pallas kernels for 0% -> 0%
where the time goes in v2:
time: 129 us
  Pallas kernels  120 us (93%)
  local copies, waits for them, and re-layouts  5.42 us (4%)
  other arithmetic  3.03 us (2%)
    pallas_call x1, Pallas kernels, on_device(): pl.pallas_call(functools.partial(layer_kernel, count, frames, mem, tile,...  120 us
    unnamed x2, local copies, waits for them, and re-layouts  3.53 us

profile of v2, /device:TPU:16, one launch (start us, length us, event | category | flops | bytes accessed | tf_op | source)
XLA Modules:
  0.0 129.1 jit_solution(8581162140764106416)
XLA Ops:
  0.7 0.1 pad.1.clone
  0.7 0.8 fusion.8
  1.5 0.1 copy.15
  1.6 0.1 copy.16
  1.7 0.7 fusion.5
  2.4 0.1 pad_maximum_fusion
  2.5 0.7 add_select_fusion.1
  3.2 0.1 eq.44
  3.3 0.1 add.89
  3.3 0.8 fusion.2
  4.1 0.1 broadcast_in_dim.53
  4.2 0.7 reshape.90.valid
  4.8 0.7 broadcast_in_dim.56.want_out
  5.6 120.0 %shard_map.104 = (bf16[128,1536]{1,0:T(8,128)(2,1)}, bf16[128,1536]{1,0:T(8,128)(2,1)}) custom-call(s32[16]{0:T(128)} %get-tuple-element.8.spots, s32[16]{0:T(128)} %get-tuple-element.7.place, f32[4,224]{1,0:T(4,128)} %reshape.90.valid, bf16[128,1536]{1,0:T(8,128)(2,1)} %bitcast.7, bf16[128,1536]{1,0:T(8,128)(2,1)} %bitcast.8, ...), custom_call_target="tpu_custom_call" | custom-call | tf_op jit(solution)/shard_map/pallas_call | solution.py:363
  125.6 1.8 %copy.19 = bf16[4,32,1536]{2,1,0:T(8,128)(2,1)} copy(bf16[4,32,1536]{2,1,0:T(8,128)(2,1)} %bitcast.6) | data formatting | bytes 786432
  127.4 1.8 %copy.20 = bf16[4,32,1536]{2,1,0:T(8,128)(2,1)} copy(bf16[4,32,1536]{2,1,0:T(8,128)(2,1)} %bitcast.5) | data formatting | bytes 786432
  (2 shorter events, 0.0 us)

commit v3 on v2

--- a/solution.py
+++ b/solution.py
@@ -25,10 +25,10 @@
 
 def layer_kernel(
     count, frames, mem, tile, head_dim, steps,
-    spots, place, valid, x_ref, cot_ref, want_out,
+    spots, place, wanted, recalled, tiles, x_ref, cot_ref,
     wq_hbm, wo_hbm, wk_hbm, wv_hbm,
     layer_ref, grad_ref,
-    weights, q_ref, g_ref, k_ext, v_ext, k_mem, v_mem, want_in, choose, rows_out, rows_in,
+    weights, q_ref, g_ref, k_ext, v_ext, k_mem, v_mem, want_out, want_in, choose, rows_out, rows_in,
     mixed, query_grad, sums, blocks, outgoing, incoming, total,
     weight_sem, want_send, want_recv, row_send, row_recv, halo_send, halo_recv,
     send_sem, recv_sem, edge_send, edge_recv,
@@ -66,6 +66,10 @@
     def _(i):
         pl.semaphore_signal(barrier, inc=1, device_id=peer(i), device_id_type=MESH)
 
+    @pl.loop(0, count)
+    def _(i):
+        want_out[i] = jnp.full((8, own), wanted[i], jnp.int32)
+
     pl.semaphore_wait(barrier, count - 1)
 
     def ask(i):
@@ -223,6 +227,16 @@
             device_id_type=MESH,
         )
 
+    block_of = lax.broadcasted_iota(jnp.int32, (1, (3 + mem) * tile), 1) // tile
+
+    def valid(f):
+        frame = me * frames + f
+        lower = jnp.where(frame >= 1, tiles[f, 0], 0)
+        upper = jnp.where(frame < frames * count - 1, tiles[f, 1], 0)
+        near = jnp.where(block_of == 0, lower, jnp.where(block_of == 1, 1, upper))
+        kept = jnp.where(block_of - 3 < recalled[f], 1, 0)
+        return jnp.where(block_of < 3, near, kept) > 0
+
     def attend(g):
         lanes = pl.ds(pl.multiple_of(g * cols, cols), cols)
         for f in range(frames):
@@ -240,7 +254,7 @@
             queries = spread(q_ref[here, lanes])
             grads = spread(g_ref[here, lanes])
             scores = dot(queries, keys, NT) * inv_root
-            scores = jnp.where(valid[f : f + 1, :] > 0.5, scores, -1e30)
+            scores = jnp.where(valid(f), scores, -1e30)
             expo = jnp.exp(scores - jnp.max(scores, axis=-1, keepdims=True))
             prob = expo / jnp.sum(expo, axis=-1, keepdims=True)
             low = prob.astype(jnp.bfloat16)
@@ -342,19 +356,7 @@
     place = jnp.sum(jnp.where(matched, entry[None, :], 0), axis=1).astype(jnp.int32)
     wanted = jnp.sum(jnp.where(matched, local + 1, 0), axis=1).astype(jnp.int32) - 1
     own = frames * tile
-    want_out = jnp.broadcast_to(
-        jnp.where(wanted < 0, -frames, wanted)[:, None, None], (count, 8, own)
-    )
-    frame_ids = jnp.arange(frames, dtype=jnp.int32)
-
-    global_ids = me * frames + frame_ids
-    lower = (tile_mask[:, 0] * (global_ids >= 1)).astype(jnp.float32)
-    upper = (tile_mask[:, 1] * (global_ids < frames * count - 1)).astype(jnp.float32)
-    kept = (jnp.arange(mem, dtype=jnp.int32)[None, :] < memory_count[:, None]).astype(jnp.float32)
-    valid = jnp.concatenate(
-        [lower[:, None], jnp.ones((frames, 1), jnp.float32), upper[:, None], kept], axis=1
-    )
-    valid = jnp.repeat(valid, tile, axis=1)
+    wanted = jnp.where(wanted < 0, -frames, wanted)
 
     vmem = pl.BlockSpec(memory_space=pltpu.VMEM)
     smem = pl.BlockSpec(memory_space=pltpu.SMEM)
@@ -362,7 +364,7 @@
     block = (2, tile, cols)
     layer_out, latent_grad = pl.pallas_call(
         functools.partial(layer_kernel, count, frames, mem, tile, head_dim, steps),
-        in_specs=[smem, smem] + [vmem] * 4 + [hbm] * 4,
+        in_specs=[smem] * 5 + [vmem] * 2 + [hbm] * 4,
         out_specs=[vmem, vmem],
         out_shape=[
             jax.ShapeDtypeStruct((own, width), jnp.bfloat16),
@@ -376,6 +378,7 @@
             pltpu.VMEM((own + 2 * tile, inner), jnp.bfloat16),
             pltpu.VMEM((count, tile, inner), jnp.bfloat16),
             pltpu.VMEM((count, tile, inner), jnp.bfloat16),
+            pltpu.VMEM((count, 8, own), jnp.int32),
             pltpu.VMEM((count, 8, own), jnp.int32),
             pltpu.VMEM(((count + 2) * tile, own), jnp.bfloat16),
             pltpu.VMEM((count, tile, width), jnp.bfloat16),
@@ -403,7 +406,7 @@
             collective_id=0, has_side_effects=True, vmem_limit_bytes=58 * 2**20
         ),
     )(
-        spots, place, valid, rows, cotangent.reshape(-1, width), want_out,
+        spots, place, wanted, memory_count, tile_mask, rows, cotangent.reshape(-1, width),
         w_query, w_out, w_key, w_value,
     )
     return (

time: 129 us -> 128 us (level)
    convert_element_type x2 -> x0, other arithmetic: 1.48 us -> none  [the longest x1 0.76 us: on_device(): lower = (tile_mask[:, 0] * (global_ids >= 1)).astype(jnp.float32)]
    unnamed x2 -> x3, local copies, waits for them, and re-layouts: 3.53 us -> 4.87 us
where the time goes in v3:
time: 128 us
  Pallas kernels  120 us (94%)
  local copies, waits for them, and re-layouts  5.04 us (4%)
  other arithmetic  1.95 us (2%)
    pallas_call x1, Pallas kernels, on_device(): pl.pallas_call(functools.partial(layer_kernel, count, frames, mem, tile,...  120 us
    unnamed x3, local copies, waits for them, and re-layouts  4.87 us

profile of v3, /device:TPU:16, one launch (start us, length us, event | category | flops | bytes accessed | tf_op | source)
XLA Modules:
  0.0 127.7 jit_solution(16175718389395708826)
XLA Ops:
  0.7 1.3 %copy.12.tiles = s32[4,2]{1,0:T(4,128)} copy(s32[4,2]{0,1:T(2,128)} %param.17) | data formatting | bytes 64 | tf_op args[8]
  2.0 0.7 add_select_fusion.1
  2.7 0.1 eq.44
  2.8 0.1 add.66
  2.8 0.8 fusion.2
  3.6 0.5 compare_select_fusion.3.wanted
  4.1 120.0 %shard_map.104 = (bf16[128,1536]{1,0:T(8,128)(2,1)}, bf16[128,1536]{1,0:T(8,128)(2,1)}) custom-call(s32[16]{0:T(128)} %get-tuple-element.8.spots, s32[16]{0:T(128)} %get-tuple-element.7.place, s32[16]{0:T(128)} %compare_select_fusion.3.wanted, s32[4]{0:T(128)} %recalled.1, s32[4,2]{1,0:T(4,128)} %copy.12.tiles, bf16[128,1536]{1,0:T(8,128)(2,1)} %bitcast.6, ...), custom_call_target="tpu_custom_call" | custom-call | tf_op jit(solution)/shard_map/pallas_call | solution.py:365
  124.1 1.8 %copy.15 = bf16[4,32,1536]{2,1,0:T(8,128)(2,1)} copy(bf16[4,32,1536]{2,1,0:T(8,128)(2,1)} %bitcast.5) | data formatting | bytes 786432
  125.9 1.8 %copy.16 = bf16[4,32,1536]{2,1,0:T(8,128)(2,1)} copy(bf16[4,32,1536]{2,1,0:T(8,128)(2,1)} %bitcast.4) | data formatting | bytes 786432
  (1 shorter events, 0.0 us)
